TPU v7x, 256 devices: a whole 4x4x8 slice. The times are simulated.
256 devices in a mesh: gx: 16 (over z_hi, x, core), gy: 16 (over z_lo, y).
Axes of the slice: x: 4, y: 4, z: 8 (z_hi: 2, z_lo: 4; z = z_hi * 4 + z_lo), core: 2. Of those that a mesh axis runs over, the one named last changes fastest.
Arguments:
- node_feats: bfloat16 [262144, 128], P(('gx', 'gy')), may hold values from -6 to 6
- radial: bfloat16 [8, 32, 262144], P(None, None, ('gx', 'gy')), may hold values from -3 to 3
- neighbours: int32 [32, 262144], P(None, ('gx', 'gy')), may hold values from 0 to 8255, as said below
- nbr_count: int32 [262144], P(('gx', 'gy')), may hold values from 8 to 32, as said below
- domain_count: int32 [256], P(('gx', 'gy')), may hold values from 256 to 1024, as said below
- base_cells: int32 [3, 262144], P(None, ('gx', 'gy')), may hold values from 0 to 255, as said below
- spline_weights: float32 [3, 4, 262144], P(None, None, ('gx', 'gy')), as said below
- w_proj: bfloat16 [2, 128, 128], replicated, may hold values from -0.5 to 0.5
- w_radial: bfloat16 [2, 8, 128], replicated, may hold values from -2 to 2
- w_mix: bfloat16 [2, 128, 128], replicated, may hold values from -0.5 to 0.5
- w_charge: bfloat16 [128], replicated, may hold values from -0.5 to 0.5
- green_kernel: float32 [256, 256, 256], P(None, 'gx', 'gy'), may hold values from 1 to 200, as said below
Outputs:
- charges: float32 [262144], P(('gx', 'gy'))
- atom_potential: float32 [262144], P(('gx', 'gy'))
- potential_grid: float32 [256, 256, 256], P('gx', 'gy')
Inputs may be any that keep to these rules, and one draw needn't show every extreme that they name: `neighbours`: an entry is r * 1024 + t (see the steps). With r = 4 (the atom's own domain, slot s), t - s lies in -128 .. 127, and t is below that domain's count if s is. Atoms of slot s < 256 may also name other domains, by the band s // 64: band 0 names r with offset -1 along gx (any offset along gy) and t from 64 to 127; band 1 names offset +1 along gx (any along gy) and t below 64; band 2 names offset (0, -1) and t from 192 to 255; band 3 names offset (0, +1) and t from 128 to 191. Other atoms name only their own domain. Slots at or past nbr_count hold entries of the same kind. `nbr_count`: slots k below the count are live. `domain_count`: the present atoms of a domain fill its first slots. `base_cells`: row 0 lies in 1 to 16, row 1 in 1 to 16, row 2 in 0 to 255. `spline_weights`: for each dimension and atom, the four cubic B-spline weights of one fraction u in [0, 1): (1-u)^3/6, (3u^3-6u^2+4)/6, (-3u^3+3u^2+3u+1)/6, u^3/6. `green_kernel`: the value at wave number k equals the value at (-k) mod 256, taken along all three dimensions.
All inputs are finite; a program needn't handle non-finite values.
Results may differ from a plain program's by a relative error of at most 0.0075.
Values may be sent and summed in bfloat16 or wider, within the bound.
A program may use at most 64 MiB of HBM per device.

v0:
```python
import functools
import math

import jax
import jax.numpy as jnp
import ml_dtypes
import numpy as np
from jax import lax
from jax.experimental import pallas as pl
from jax.experimental.pallas import tpu as pltpu
from jax.sharding import PartitionSpec as P

K = 32
L = 2


MESH = pl.DeviceIdType.MESH
TN = (((0,), (0,)), ((), ()))
NT = (((1,), (1,)), ((), ()))
NN = (((1,), (0,)), ((), ()))


def dot(a, b, dims=NN):
    return lax.dot_general(a, b, dims, preferred_element_type=jnp.float32)


def ring(index, step, count):
    return lax.rem(index + step + count, count)


def message_kernel(
    num_x,
    num_y,
    feats_ref,
    radial_ref,
    nbr_ref,
    count_ref,
    fill_ref,
    proj_ref,
    filt_ref,
    mix_ref,
    charge_w_ref,
    charges_ref,
    state,
    table,
    rows_out,
    rows_in,
    head_a,
    head_b,
    pick,
    filt_k,
    total,
    send_sem,
    recv_sem,
):
    px, py = lax.axis_index("gx"), lax.axis_index("gy")
    barrier = pltpu.get_barrier_semaphore()
    peers = [(dx, dy) for dx in (-1, 0, 1) for dy in (-1, 0, 1) if (dx, dy) != (0, 0)]
    for dx, dy in peers:
        pl.semaphore_signal(
            barrier,
            inc=1,
            device_id=(ring(px, dx, num_x), ring(py, dy, num_y)),
            device_id_type=MESH,
        )
    code = nbr_ref[...]
    direction, slot = code // 1024, code % 1024
    lane = lax.broadcasted_iota(jnp.int32, (K, 1024), 1)
    live = lax.broadcasted_iota(jnp.int32, (K, 1024), 0) < count_ref[...]
    block = lane // 128
    near = slot - jnp.maximum(block - 1, 0) * 128
    far = jnp.where(
        direction < 3,
        192 + direction * 64 + slot,
        jnp.where(
            direction > 5,
            64 + direction * 64 + slot,
            jnp.where(direction == 3, 192 + slot, 320 + slot),
        ),
    )
    named = jnp.where(live, jnp.where(direction == 4, near, far), -8192).astype(jnp.float32)
    for b in range(8):
        pick[:, b, :] = named[:, b * 128 : (b + 1) * 128]

    state[...] = jnp.transpose(feats_ref[...].astype(jnp.float32))
    row_id = lax.broadcasted_iota(jnp.int32, (128, 128), 0).astype(jnp.bfloat16)
    one, zero = jnp.ones((128, 128), jnp.bfloat16), jnp.zeros((128, 128), jnp.bfloat16)
    basis_k = lax.broadcasted_iota(jnp.int32, (128, 8 * K), 1) % K

    def onehot(k, begin, groups):
        row = pick[k, begin // 128 : begin // 128 + 1, :]
        parts = [
            jnp.where(row_id == jnp.broadcast_to((row - 128.0 * g).astype(jnp.bfloat16), (128, 128)), one, zero)
            for g in range(groups)
        ]
        return jnp.concatenate(parts, axis=0)

    def messages(group, tables):
        begin = group * 256
        radial = radial_ref[:, begin : begin + 256]
        total[...] = jnp.zeros_like(total)

        def step(pair, carry):
            k = 2 * pair
            filters = dot(filt_k[pl.ds(pl.multiple_of(k * 128, 256), 256), :], radial)
            for half, (source, groups) in enumerate(tables):
                at = begin + 128 * half
                hot = jnp.concatenate([onehot(k, at, groups), onehot(k + 1, at, groups)], axis=1)
                got = dot(source(), hot)
                lanes = slice(128 * half, 128 * half + 128)
                total[:, lanes] += (
                    got[:, :128] * filters[:128, lanes] + got[:, 128:] * filters[128:, lanes]
                )
            return carry

        lax.fori_loop(0, K // 2, step, 0, unroll=2)
        return (total[...] * (1.0 / math.sqrt(K))).astype(jnp.bfloat16)

    for layer in range(L):
        spread = jnp.concatenate(
            [jnp.broadcast_to(filt_ref[layer, b], (K, 128)) for b in range(8)], axis=0
        )
        spread = jnp.transpose(spread.astype(jnp.float32))
        for k in range(K):
            filt_k[k * 128 : (k + 1) * 128, :] = jnp.where(basis_k == k, spread, 0.0).astype(jnp.bfloat16)
        proj = proj_ref[layer]
        first = dot(proj, state[:, :256].astype(jnp.bfloat16), TN).astype(jnp.bfloat16)
        rows_out[layer] = jnp.transpose(first.astype(jnp.float32)).astype(jnp.bfloat16)
        if layer == 0:
            pl.semaphore_wait(barrier, 8)
        copies = []
        for dx, dy in peers:
            if dx == 1:
                band, land = 1, 1 - dy
            elif dx == -1:
                band, land = 0, 4 - dy
            elif dy == 1:
                band, land = 3, 6
            else:
                band, land = 2, 7
            copies.append(
                pltpu.make_async_remote_copy(
                    src_ref=rows_out.at[layer, pl.ds(band * 64, 64)],
                    dst_ref=rows_in.at[layer, pl.ds(land * 64, 64)],
                    send_sem=send_sem.at[layer, land],
                    recv_sem=recv_sem.at[layer, land],
                    device_id=(ring(px, dx, num_x), ring(py, dy, num_y)),
                    device_id_type=MESH,
                )
            )
            copies[-1].start()
        table[:, :256] = first
        table[:, 256:] = dot(proj, state[:, 256:].astype(jnp.bfloat16), TN).astype(jnp.bfloat16)

        def update(group, tables):
            begin = group * 256
            u = messages(group, tables)
            mixed = dot(mix_ref[layer], u, TN)
            lanes = slice(begin, begin + 256)
            state[:, lanes] = (
                (state[:, lanes] + mixed / (1.0 + jnp.exp(-mixed))).astype(jnp.bfloat16).astype(jnp.float32)
            )

        def window(block):
            low = max(block - 1, 0) * 128
            high = min(block + 2, 8) * 128
            return (lambda: table[:, low:high]), (high - low) // 128

        for group in (1, 2, 3):
            update(group, [window(2 * group), window(2 * group + 1)])
        for copy in copies:
            copy.wait()
        far_rows = jnp.transpose(rows_in[layer].astype(jnp.float32)).astype(jnp.bfloat16)
        head_a[:, :256] = table[:, :256]
        head_a[:, 256:] = far_rows[:, :384]
        head_b[:, :384] = table[:, :384]
        head_b[:, 384:] = far_rows[:, 384:]
        update(0, [((lambda: head_a[...]), 5), ((lambda: head_b[...]), 4)])
    charge = dot(charge_w_ref[...], state[...].astype(jnp.bfloat16))[0:1]
    inside = lax.broadcasted_iota(jnp.int32, (1, 1024), 1) < fill_ref[...]
    charges_ref[...] = jnp.where(inside, charge, 0.0)


def message_passing(feats, radial, neighbours, nbr_count, fill, w_proj, w_radial, w_mix, w_charge):
    num_x, num_y = lax.axis_size("gx"), lax.axis_size("gy")
    vmem = pl.BlockSpec(memory_space=pltpu.VMEM)
    bf16 = jnp.bfloat16
    return pl.pallas_call(
        functools.partial(message_kernel, num_x, num_y),
        out_shape=jax.ShapeDtypeStruct((1, 1024), jnp.float32),
        in_specs=[vmem] * 9,
        out_specs=vmem,
        scratch_shapes=[
            pltpu.VMEM((128, 1024), jnp.float32),
            pltpu.VMEM((128, 1024), bf16),
            pltpu.VMEM((L, 256, 128), bf16),
            pltpu.VMEM((L, 512, 128), bf16),
            pltpu.VMEM((128, 640), bf16),
            pltpu.VMEM((128, 512), bf16),
            pltpu.VMEM((K, 8, 128), jnp.float32),
            pltpu.VMEM((K * 128, 8 * K), bf16),
            pltpu.VMEM((128, 256), jnp.float32),
            pltpu.SemaphoreType.DMA((L, 8)),
            pltpu.SemaphoreType.DMA((L, 8)),
        ],
        compiler_params=pltpu.CompilerParams(
            collective_id=0, has_side_effects=True, vmem_limit_bytes=48 * 1024 * 1024
        ),
        name="message_passing",
    )(
        feats,
        radial.reshape(8 * K, 1024),
        neighbours,
        nbr_count.reshape(1, 1024),
        fill,
        w_proj,
        w_radial.reshape(L, 8, 1, 128),
        w_mix,
        jnp.broadcast_to(w_charge.reshape(1, 128), (8, 128)),
    )

SIDES = ((-1, 0), (1, 0), (0, -1), (0, 1), (-1, -1), (-1, 1), (1, -1), (1, 1))
SIDE_ROWS = (32, 32, 32, 32, 16, 16, 16, 16)
SIDE_AT = (0, 32, 64, 96, 128, 144, 160, 176)
OPPOSITE = (1, 0, 3, 2, 7, 6, 5, 4)


def split(values):
    high = values.astype(jnp.bfloat16)
    return high, (values - high.astype(jnp.float32)).astype(jnp.bfloat16)


def np_split(values):
    high = values.astype(ml_dtypes.bfloat16)
    return high, (values - high.astype(np.float64)).astype(ml_dtypes.bfloat16)


def mesh_tables():
    ids = np.arange(256)
    angles = 2.0 * np.pi * (ids[:, None] * ids[None, :] % 256) / 256
    waves = np.concatenate([np.cos(angles), np.sin(angles)], axis=0)
    column, slot = np.arange(16)[:, None], np.arange(8)[None, :]
    kz = (16 * column + slot + (column >= 8)).reshape(128)
    turn = 2.0 * np.pi * (kz[:, None] * ids[None, :] % 256) / 256
    ahead = np.stack([np.cos(turn), -np.sin(turn)])
    back = 2.0 * ahead
    ahead[0, 0], ahead[1, 0] = 1.0, 1.0 - 2.0 * (ids % 2)
    back[0, 0], back[1, 0] = ahead[0, 0], ahead[1, 0]
    back = back / 256.0**3
    fold = np.zeros((16, 16, 192))
    for at, (dx, dy) in zip(SIDE_AT, SIDES, strict=True):
        first_x, first_y = (14 if dx > 0 else 0), (14 if dy > 0 else 0)
        for i in range(2):
            if dy == 0:
                for y in range(16):
                    fold[y, first_x + i, at + 16 * i + y] = 1
            elif dx == 0:
                for x in range(16):
                    fold[first_y + i, x, at + 16 * i + x] = 1
            else:
                for j in range(2):
                    fold[first_y + j, first_x + i, at + 2 * i + j] = 1
    return (
        *np_split(waves),
        *np_split(ahead.reshape(256, 256)),
        *np_split(back.reshape(256, 256)),
        fold.reshape(256, 192).astype(ml_dtypes.bfloat16),
    )


def regroup(parts):
    group = lax.broadcasted_iota(jnp.int32, (16, 128), 1) // 16
    parts = list(parts)
    for step in (1, 2, 4):
        low = (group & step) == 0
        for i in range(8):
            if i & step == 0:
                a, b = parts[i], parts[i | step]
                parts[i] = jnp.where(low, a, pltpu.roll(b, 16 * step, 1))
                parts[i | step] = jnp.where(low, pltpu.roll(a, 128 - 16 * step, 1), b)
    return parts


def swap_groups(values):
    row = lax.broadcasted_iota(jnp.int32, values.shape, 1)
    group = lax.broadcasted_iota(jnp.int32, values.shape, 2) // 16
    for step in (1, 2, 4):
        row_high, group_high = (row & step) != 0, (group & step) != 0
        if step == 4:
            moved = pltpu.roll(pltpu.roll(values, 4, 1), 64, 2)
        else:
            up = pltpu.roll(pltpu.roll(values, 8 - step, 1), 16 * step, 2)
            down = pltpu.roll(pltpu.roll(values, step, 1), 128 - 16 * step, 2)
            moved = jnp.where(row_high, down, up)
        values = jnp.where(row_high == group_high, values, moved)
    return values


def profile(cells, base, weights):
    total = jnp.zeros(cells.shape, jnp.float32)
    for offset in range(4):
        total = total + jnp.where(cells == base[offset], weights[offset], 0.0)
    return total


def mesh_kernel(
    charges_ref,
    fill_ref,
    base_ref,
    spline_ref,
    green_ref,
    green_last_ref,
    wave_h,
    wave_l,
    ahead_h,
    ahead_l,
    back_h,
    back_l,
    fold_ref,
    atom_ref,
    grid_ref,
    plane,
    prof_h,
    prof_l,
    halo_out,
    halo_in,
    z_out,
    z_in,
    y_out,
    y_in,
    x_out,
    x_in,
    v_out,
    v_in,
    shared,
    green_in,
    send_sem,
    recv_sem,
):
    count = 16
    px, py = lax.axis_index("gx"), lax.axis_index("gy")
    barrier = pltpu.get_barrier_semaphore()

    def greet(d, carry):
        for where in ((ring(px, d, count), py), (px, ring(py, d, count))):
            pl.semaphore_signal(barrier, inc=1, device_id=where, device_id_type=MESH)
        return carry

    lax.fori_loop(1, count, greet, 0)
    for dx, dy in SIDES[4:]:
        pl.semaphore_signal(
            barrier,
            inc=1,
            device_id=(ring(px, dx, count), ring(py, dy, count)),
            device_id_type=MESH,
        )

    def remote(source, target, stage, index, where):
        return pltpu.make_async_remote_copy(
            src_ref=source,
            dst_ref=target,
            send_sem=send_sem.at[stage, index],
            recv_sem=recv_sem.at[stage, index],
            device_id=where,
            device_id_type=MESH,
        )

    def exchange(make):
        def start(d, carry):
            make(d).start()
            return carry

        lax.fori_loop(1, count, start, 0)

    def arrive(make):
        def wait(d, carry):
            make(d).wait()
            return carry

        lax.fori_loop(1, count, wait, 0)

    def side_copies(half):
        return [
            remote(
                halo_out.at[half, pl.ds(SIDE_AT[e], SIDE_ROWS[e])],
                halo_in.at[half, pl.ds(SIDE_AT[OPPOSITE[e]], SIDE_ROWS[e])],
                half,
                e,
                (ring(px, SIDES[e][0], count), ring(py, SIDES[e][1], count)),
            )
            for e in range(8)
        ]

    def column_copy(out, into, stage):
        def make(d):
            to = ring(py, d, count)
            return remote(out.at[:, to], into.at[:, py], stage, d, (px, to))

        return make

    def row_copy(out, into, stage, layers):
        def make(d):
            to = ring(px, d, count)
            return remote(out.at[layers, to], into.at[layers, px], stage, d, (to, py))

        return make

    main, extra = pl.ds(0, 2), pl.ds(2, 1)

    def green_copy():
        return remote(green_last_ref, green_in, 8, 0, (px, 0))

    def rows(dim):
        base = base_ref[dim : dim + 1, :]
        cells = [base + offset for offset in range(4)]
        if dim == 2:
            cells = [jnp.where(c >= 256, c - 256, c) for c in cells]
        return cells, [spline_ref[4 * dim + o : 4 * dim + o + 1, :] for o in range(4)]

    z_cells = lax.broadcasted_iota(jnp.int32, (256, 1024), 0)
    high, low = split(profile(z_cells, *rows(2)))
    prof_h[...] = high
    prof_l[...] = low
    sixteen = lax.broadcasted_iota(jnp.int32, (16, 1024), 0)
    eight = lax.broadcasted_iota(jnp.int32, (8, 1024), 0)
    edge = jnp.where(eight < 2, eight, eight + 16)
    in_x, in_y = (profile(sixteen + 2, *rows(dim)) for dim in (0, 1))
    edge_x, edge_y = (profile(edge, *rows(dim)) for dim in (0, 1))
    for y in range(16):
        plane[16 * y : 16 * y + 16, :] = in_y[y : y + 1, :] * in_x
    for i in range(4):
        at = 256 + 32 * (i // 2) + 16 * (i % 2)
        plane[at : at + 16, :] = edge_x[i : i + 1, :] * in_y
        plane[at + 64 : at + 80, :] = edge_y[i : i + 1, :] * in_x
    corner = sixteen < 4
    corner_x = [
        profile(jnp.where(corner, sixteen // 2 + begin, 99), *rows(0)) for begin in (0, 18)
    ]
    corner_y = [
        profile(jnp.where(corner, sixteen % 2 + begin, 99), *rows(1)) for begin in (0, 18)
    ]
    for e in range(4):
        at = 256 + SIDE_AT[4 + e]
        plane[at : at + 16, :] = corner_x[e // 2] * corner_y[e % 2]

    high, low = split(plane[...] * charges_ref[...])
    spread = dot(high, prof_h[...], NT) + dot(low, prof_h[...], NT) + dot(high, prof_l[...], NT)
    halo_out[0] = spread[256:].astype(jnp.bfloat16)
    pl.semaphore_wait(barrier, 34)
    copies = side_copies(0)
    for copy in copies:
        copy.start()

    @pl.when(py == 8)
    def _():
        green_copy().start()

    for copy in copies:
        copy.wait()
    high, low = split(spread[:256] + dot(fold_ref[...], halo_in[0]))

    lines = dot(ahead_h[...], high, NT) + dot(ahead_l[...], high, NT) + dot(ahead_h[...], low, NT)
    halves = [
        swap_groups(lines[:, 128 * half : 128 * half + 128].reshape(32, 8, 128)) for half in (0, 1)
    ]
    z_out[...] = jnp.concatenate(halves, axis=1).astype(jnp.bfloat16).reshape(2, 16, 16, 128)
    make = column_copy(z_out, z_in, 2)
    exchange(make)
    z_in[:, pl.ds(py, 1)] = z_out[:, pl.ds(py, 1)]
    arrive(make)

    cos_h, sin_h = wave_h[:256], wave_h[256:]
    cos_l, sin_l = wave_l[:256], wave_l[256:]
    both = jnp.concatenate([z_in[0].reshape(256, 128), z_in[1].reshape(256, 128)], axis=1)
    both = jnp.transpose(both.astype(jnp.float32)).astype(jnp.bfloat16)
    c = dot(both, cos_h) + dot(both, cos_l)
    s = dot(both, sin_h) + dot(both, sin_l)
    apart = (lax.broadcasted_iota(jnp.int32, (128, 256), 0) < 16) & (py == 0)
    real = c[:128] + jnp.where(apart, 0.0, s[128:])
    imag = jnp.where(apart, 0.0, c[128:]) - s[:128]

    def to_slots(values, layer):
        for half in (0, 1):
            lanes = slice(128 * half, 128 * half + 128)
            done = regroup([values[16 * i : 16 * i + 16, lanes] for i in range(8)])
            for i in range(8):
                y_out[layer, 8 * half + i] = done[i].astype(jnp.bfloat16)

    to_slots(real, 0)
    to_slots(imag, 1)
    make = row_copy(y_out, y_in, 3, main)
    exchange(make)
    y_in[0:2, pl.ds(px, 1)] = y_out[0:2, pl.ds(px, 1)]

    @pl.when(py == 0)
    def _():
        blank = jnp.zeros((96, 256), jnp.float32)
        to_slots(jnp.concatenate([c[128:144], -s[128:144], blank], axis=0), 2)
        exchange(row_copy(y_out, y_in, 4, extra))
        y_in[2:3, pl.ds(px, 1)] = y_out[2:3, pl.ds(px, 1)]

    arrive(make)

    def forward_x(values):
        return dot(cos_h, values) + dot(cos_l, values), dot(sin_h, values) + dot(sin_l, values)

    def inverse_x(values):
        high, low = split(values)
        return (
            dot(cos_h, high) + dot(cos_l, high) + dot(cos_h, low),
            dot(sin_h, high) + dot(sin_l, high) + dot(sin_h, low),
        )

    c, s = forward_x(
        jnp.concatenate([y_in[0].reshape(256, 128), y_in[1].reshape(256, 128)], axis=1)
    )
    real = (c[:, :128] + s[:, 128:]) * green_ref[...]
    imag = (c[:, 128:] - s[:, :128]) * green_ref[...]
    c, s = inverse_x(jnp.concatenate([real, imag], axis=1))
    x_out[0] = (c[:, :128] - s[:, 128:]).astype(jnp.bfloat16).reshape(16, 16, 128)
    x_out[1] = (c[:, 128:] + s[:, :128]).astype(jnp.bfloat16).reshape(16, 16, 128)
    make = row_copy(x_out, x_in, 5, main)
    exchange(make)
    x_in[0:2, pl.ds(px, 1)] = x_out[0:2, pl.ds(px, 1)]

    @pl.when(py == 0)
    def _():
        arrive(row_copy(y_out, y_in, 4, extra))
        green_copy().wait_recv()
        first = lax.broadcasted_iota(jnp.int32, (256, 128), 1) < 16
        c, s = forward_x(y_in[2].reshape(256, 128))
        real = (c + pltpu.roll(s, 112, 1)) * green_in[...]
        imag = (pltpu.roll(c, 112, 1) - s) * green_in[...]
        c, s = inverse_x(real + pltpu.roll(imag, 16, 1))
        real = jnp.where(first, c - pltpu.roll(s, 112, 1), 0.0)
        imag = jnp.where(first, pltpu.roll(c, 112, 1) + s, 0.0)
        x_out[2] = (real + pltpu.roll(imag, 16, 1)).astype(jnp.bfloat16).reshape(16, 16, 128)
        back_copy = row_copy(x_out, x_in, 6, extra)
        exchange(back_copy)
        x_in[2:3, pl.ds(px, 1)] = x_out[2:3, pl.ds(px, 1)]

    @pl.when(py == 8)
    def _():
        green_copy().wait_send()

    arrive(make)

    def to_rows(layer):
        halves = [
            regroup([x_in[layer, 8 * half + i].astype(jnp.float32) for i in range(8)])
            for half in (0, 1)
        ]
        return [jnp.concatenate([halves[0][i], halves[1][i]], axis=1) for i in range(8)]

    real, imag = to_rows(0), to_rows(1)
    shared[0] = real[0]
    shared[1] = imag[0]

    @pl.when(py == 0)
    def _():
        arrive(row_copy(x_out, x_in, 6, extra))
        last = to_rows(2)
        shared[0] = -last[1]
        shared[1] = last[0]

    a = jnp.concatenate(real, axis=0).astype(jnp.bfloat16)
    b = jnp.concatenate(imag, axis=0).astype(jnp.bfloat16)
    a_too = jnp.concatenate([shared[0], *real[1:]], axis=0).astype(jnp.bfloat16)
    b_too = jnp.concatenate([shared[1], *imag[1:]], axis=0).astype(jnp.bfloat16)
    real = dot(cos_h, a, NT) + dot(cos_l, a, NT) - dot(sin_h, b, NT) - dot(sin_l, b, NT)
    imag = dot(cos_h, b_too, NT) + dot(cos_l, b_too, NT) + dot(sin_h, a_too, NT) + dot(sin_l, a_too, NT)
    v_out[0] = real.astype(jnp.bfloat16).reshape(16, 16, 128)
    v_out[1] = imag.astype(jnp.bfloat16).reshape(16, 16, 128)
    make = column_copy(v_out, v_in, 7)
    exchange(make)
    v_in[:, pl.ds(py, 1)] = v_out[:, pl.ds(py, 1)]
    arrive(make)

    got = v_in[...].reshape(32, 16, 128).astype(jnp.float32)
    halves = [swap_groups(got[:, 8 * half : 8 * half + 8]).reshape(256, 128) for half in (0, 1)]
    lines = jnp.concatenate(halves, axis=1).astype(jnp.bfloat16)
    grid = dot(lines, back_h[...], TN) + dot(lines, back_l[...], TN)
    grid_ref[...] = grid
    high, low = split(grid)
    halo_out[1] = dot(fold_ref[...], high, TN).astype(jnp.bfloat16)
    copies = side_copies(1)
    for copy in copies:
        copy.start()

    sampled = dot(high, prof_h[...]) + dot(low, prof_h[...]) + dot(high, prof_l[...])
    total = jnp.sum(sampled * plane[:256], axis=0, keepdims=True)
    for copy in copies:
        copy.wait()
    sampled = dot(halo_in[1], prof_h[...]) + dot(halo_in[1], prof_l[...])
    total = total + jnp.sum(sampled * plane[256:], axis=0, keepdims=True)
    inside = lax.broadcasted_iota(jnp.int32, (1, 1024), 1) < fill_ref[...]
    atom_ref[...] = jnp.where(inside, total, 0.0)


def mesh_potential(charges, fill, base_cells, spline_weights, green):
    vmem = pl.BlockSpec(memory_space=pltpu.VMEM)
    bf16, f32 = jnp.bfloat16, jnp.float32
    picked = jnp.where(lax.axis_index("gy") < 8, green[:, :, 0:8], green[:, :, 1:9])
    picked = jnp.transpose(picked, (0, 2, 1)).reshape(256, 128)
    last = jnp.pad(green[:, :, 0], ((0, 0), (0, 112)))
    blocks = (16, 16, 128)
    atom, grid = pl.pallas_call(
        mesh_kernel,
        out_shape=(
            jax.ShapeDtypeStruct((1, 1024), f32),
            jax.ShapeDtypeStruct((256, 256), f32),
        ),
        in_specs=[vmem] * 13,
        out_specs=(vmem, vmem),
        scratch_shapes=[
            pltpu.VMEM((448, 1024), f32),
            pltpu.VMEM((256, 1024), bf16),
            pltpu.VMEM((256, 1024), bf16),
            pltpu.VMEM((2, 192, 256), bf16),
            pltpu.VMEM((2, 192, 256), bf16),
            pltpu.VMEM((2, *blocks), bf16),
            pltpu.VMEM((2, *blocks), bf16),
            pltpu.VMEM((3, *blocks), bf16),
            pltpu.VMEM((3, *blocks), bf16),
            pltpu.VMEM((3, *blocks), bf16),
            pltpu.VMEM((3, *blocks), bf16),
            pltpu.VMEM((2, *blocks), bf16),
            pltpu.VMEM((2, *blocks), bf16),
            pltpu.VMEM((2, 16, 256), f32),
            pltpu.VMEM((256, 128), f32),
            pltpu.SemaphoreType.DMA((9, 16)),
            pltpu.SemaphoreType.DMA((9, 16)),
        ],
        compiler_params=pltpu.CompilerParams(
            collective_id=1, has_side_effects=True, vmem_limit_bytes=48 * 1024 * 1024
        ),
        name="mesh_potential",
    )(
        charges,
        fill,
        base_cells,
        spline_weights.reshape(12, 1024),
        picked,
        last,
        *(jnp.asarray(table) for table in mesh_tables()),
    )
    return atom, jnp.transpose(grid.reshape(16, 16, 256), (1, 0, 2))


def shards(
    node_feats,
    radial,
    neighbours,
    nbr_count,
    domain_count,
    base_cells,
    spline_weights,
    w_proj,
    w_radial,
    w_mix,
    w_charge,
    green_kernel,
):
    fill = jnp.broadcast_to(domain_count.reshape(1, 1), (1, 1024))
    charges = message_passing(
        node_feats, radial, neighbours, nbr_count, fill, w_proj, w_radial, w_mix, w_charge
    )
    atom_potential, potential = mesh_potential(
        charges, fill, base_cells, spline_weights, green_kernel
    )
    return (charges.reshape(1024), atom_potential.reshape(1024), potential)


def solution(mesh):
    return jax.shard_map(
        shards,
        mesh=mesh,
        in_specs=(
            P(("gx", "gy"), None),
            P(None, None, ("gx", "gy")),
            P(None, ("gx", "gy")),
            P(("gx", "gy")),
            P(("gx", "gy")),
            P(None, ("gx", "gy")),
            P(None, None, ("gx", "gy")),
            P(),
            P(),
            P(),
            P(),
            P(None, "gx", "gy"),
        ),
        out_specs=(P(("gx", "gy")), P(("gx", "gy")), P("gx", "gy", None)),
        check_vma=False,
    )
```

profile of v0, /device:TPU:1, one launch (start us, length us, event | category | flops | bytes accessed | tf_op | source)
XLA Modules:
  0.0 97.0 jit_solution(12159137731761015152)
XLA Ops:
  0.6 0.0 copy-start
  0.6 1.1 %fusion = (f32[256,16,8]{0,2,1:T(8,128)S(1)}, f32[256,16,8]{0,2,1:T(8,128)S(1)}) fusion(f32[256,16,16]{0,2,1:T(8,128)} %param.30), kind=kLoop, calls=%fused_computation.2 | loop fusion | bytes 524288 | tf_op jit(solution)/shard_map/slice | solution.py:603
  1.7 0.0 copy-start.1
  1.8 0.1 copy_select_fusion
  1.8 0.0 copy-start.9
  1.9 0.0 copy-start.10
  1.9 0.0 copy-start.11
  1.9 0.1 copy.29.green_ref
  2.6 0.0 copy-start.15
  2.7 0.7 copy-done.15
  3.3 0.0 copy-start.16
  3.3 0.6 copy-done.16
  4.0 0.0 copy-start.13
  4.0 0.0 copy-done
  4.0 0.0 copy-done.1
  4.0 0.0 copy-done.9
  4.0 0.0 copy-done.10
  4.0 0.0 copy-done.11
  4.0 0.6 copy-done.13
  4.7 0.0 copy-start.14
  4.7 0.0 copy-start.4
  4.7 0.0 copy-start.5
  4.7 0.0 copy-start.6
  4.7 0.0 copy-start.7
  4.7 0.0 copy-start.8
  4.7 37.5 %message_passing.1.charges_ref = f32[1,1024]{1,0:T(1,128)S(1)} custom-call(bf16[1024,128]{1,0:T(8,128)(2,1)S(1)} %copy-done.1, bf16[256,1024]{1,0:T(8,128)(2,1)S(1)} %bitcast.15, s32[32,1024]{1,0:T(8,128)S(1)} %copy-done.9, s32[1,1024]{1,0:T(1,128)S(1)} %bitcast.18, s32[1,1024]{1,0:T(1,128)S(1)} %broadcast_in_dim.13.fill_ref, ...), custom_call_target="tpu_custom_call" | custom-call | tf_op jit(solution)/shard_map/message_passing/pallas_call | solution.py:188
  42.2 0.0 copy-start.12
  42.2 0.9 slice.11
  43.1 0.0 copy-start.2
  43.1 0.0 copy-start.3
  43.1 0.1 copy.33
  43.3 0.0 copy-done.14
  43.3 0.0 copy-done.4
  43.3 0.0 copy-done.5
  43.3 0.0 copy-done.6
  43.3 0.0 copy-done.7
  43.3 0.0 copy-done.8
  43.4 0.0 copy-done.12
  43.4 0.7 copy-done.2
  44.1 0.1 copy-done.3
  44.2 50.8 %mesh_potential.1 = (f32[1,1024]{1,0:T(1,128)S(1)}, f32[256,256]{1,0:T(8,128)S(1)}) custom-call(f32[1,1024]{1,0:T(1,128)S(1)} %message_passing.1.charges_ref, s32[1,1024]{1,0:T(1,128)S(1)} %broadcast_in_dim.13.fill_ref, s32[3,1024]{1,0:T(4,128)S(1)} %copy-done.12, f32[12,1024]{1,0:T(8,128)S(1)} %reshape.40.spline_ref, f32[256,128]{1,0:T(8,128)S(1)} %copy.29.green_ref, ...), custom_call_target="tpu_custom_call" | custom-call | tf_op jit(solution)/shard_map/mesh_potential/pallas_call | solution.py:607
  95.0 0.9 copy.37
  95.8 0.6 copy.41
  96.4 0.6 copy.42
  (5 shorter events, 0.0 us)
Async XLA Ops:
  0.6 3.4 %copy-start = (bf16[8,32,1024]{2,1,0:T(8,128)(2,1)S(1)}, bf16[8,32,1024]{2,1,0:T(8,128)(2,1)}, u32[]{:S(2)}) copy-start(bf16[8,32,1024]{2,1,0:T(8,128)(2,1)} %param.20) | copy-start | bytes 1572868
  1.7 2.2 %copy-start.1 = (bf16[1024,128]{1,0:T(8,128)(2,1)S(1)}, bf16[1024,128]{1,0:T(8,128)(2,1)}, u32[]{:S(2)}) copy-start(bf16[1024,128]{1,0:T(8,128)(2,1)} %feats_ref.1) | copy-start | bytes 786436
  1.8 2.2 %copy-start.9 = (s32[32,1024]{1,0:T(8,128)S(1)}, s32[32,1024]{1,0:T(8,128)}, u32[]{:S(2)}) copy-start(s32[32,1024]{1,0:T(8,128)} %nbr_ref.1) | copy-start | bytes 393220
  1.9 2.1 %copy-start.10 = (bf16[2,128,128]{2,1,0:T(8,128)(2,1)S(1)}, bf16[2,128,128]{2,1,0:T(8,128)(2,1)}, u32[]{:S(2)}) copy-start(bf16[2,128,128]{2,1,0:T(8,128)(2,1)} %proj_ref.1) | copy-start | bytes 196612
  1.9 2.1 %copy-start.11 = (bf16[2,128,128]{2,1,0:T(8,128)(2,1)S(1)}, bf16[2,128,128]{2,1,0:T(8,128)(2,1)}, u32[]{:S(2)}) copy-start(bf16[2,128,128]{2,1,0:T(8,128)(2,1)} %mix_ref.1) | copy-start | bytes 196612
  2.6 0.7 copy-start.15
  3.3 0.7 copy-start.16
  4.0 0.7 copy-start.13
  4.7 38.6 %copy-start.14 = (f32[3,4,1024]{2,1,0:T(4,128)S(1)}, f32[3,4,1024]{2,1,0:T(4,128)}, u32[]{:S(2)}) copy-start(f32[3,4,1024]{2,1,0:T(4,128)} %param.25) | copy-start | bytes 147460
  4.7 38.6 %copy-start.4 = (bf16[256,256]{1,0:T(8,128)(2,1)S(1)}, bf16[256,256]{1,0:T(8,128)(2,1)}, u32[]{:S(2)}) copy-start(bf16[256,256]{1,0:T(8,128)(2,1)} %constant.25.clone.ahead_h) | copy-start | bytes 393220
  4.7 38.6 %copy-start.5 = (bf16[256,256]{1,0:T(8,128)(2,1)S(1)}, bf16[256,256]{1,0:T(8,128)(2,1)}, u32[]{:S(2)}) copy-start(bf16[256,256]{1,0:T(8,128)(2,1)} %constant.26.clone.ahead_l) | copy-start | bytes 393220
  4.7 38.6 %copy-start.6 = (bf16[256,256]{1,0:T(8,128)(2,1)S(1)}, bf16[256,256]{1,0:T(8,128)(2,1)}, u32[]{:S(2)}) copy-start(bf16[256,256]{1,0:T(8,128)(2,1)} %constant.27.clone.back_h) | copy-start | bytes 393220
  4.7 38.7 %copy-start.7 = (bf16[256,256]{1,0:T(8,128)(2,1)S(1)}, bf16[256,256]{1,0:T(8,128)(2,1)}, u32[]{:S(2)}) copy-start(bf16[256,256]{1,0:T(8,128)(2,1)} %constant.28.clone.back_l) | copy-start | bytes 393220
  4.7 38.7 %copy-start.8 = (bf16[256,192]{1,0:T(8,128)(2,1)S(1)}, bf16[256,192]{1,0:T(8,128)(2,1)}, u32[]{:S(2)}) copy-start(bf16[256,192]{1,0:T(8,128)(2,1)} %constant.29.clone.fold_ref) | copy-start | bytes 294916
  42.2 1.2 %copy-start.12 = (s32[3,1024]{1,0:T(4,128)S(1)}, s32[3,1024]{1,0:T(4,128)}, u32[]{:S(2)}) copy-start(s32[3,1024]{1,0:T(4,128)} %base_ref.1) | copy-start | bytes 36868
  43.1 1.0 copy-start.2
  43.1 1.0 %copy-start.3 = (bf16[512,256]{1,0:T(8,128)(2,1)S(1)}, bf16[512,256]{1,0:T(8,128)(2,1)}, u32[]{:S(2)}) copy-start(bf16[512,256]{1,0:T(8,128)(2,1)} %constant.24.clone.wave_l) | copy-start | bytes 786436
where the time goes:
time: 97.3 us; the launch traced here: 97 us
  Pallas kernels  88.3 us (91%)
  local copies, waits for them, and re-layouts  7.12 us (7%)
  between operations  1.53 us (2%)
    pallas_call x1, Pallas kernels, mesh_potential(): pl.pallas_call(mesh_kernel, out_shape=(jax.ShapeDtypeStruct((1, 1024), f3...  50.8 us
    pallas_call x1, Pallas kernels, message_passing(): pl.pallas_call(functools.partial(message_kernel, num_x, num_y), out_shape...  37.5 us
    unnamed x37, local copies, waits for them, and re-layouts  4.11 us

commit v1 on v0

--- a/solution.py
+++ b/solution.py
@@ -100,9 +100,8 @@
         radial = radial_ref[:, begin : begin + 256]
         total[...] = jnp.zeros_like(total)
 
-        def step(pair, carry):
-            k = 2 * pair
-            filters = dot(filt_k[pl.ds(pl.multiple_of(k * 128, 256), 256), :], radial)
+        for k in range(0, K, 2):
+            filters = dot(filt_k[k * 128 : k * 128 + 256, :], radial)
             for half, (source, groups) in enumerate(tables):
                 at = begin + 128 * half
                 hot = jnp.concatenate([onehot(k, at, groups), onehot(k + 1, at, groups)], axis=1)
@@ -111,9 +110,6 @@
                 total[:, lanes] += (
                     got[:, :128] * filters[:128, lanes] + got[:, 128:] * filters[128:, lanes]
                 )
-            return carry
-
-        lax.fori_loop(0, K // 2, step, 0, unroll=2)
         return (total[...] * (1.0 / math.sqrt(K))).astype(jnp.bfloat16)
 
     for layer in range(L):

time: 97.3 us -> 87.5 us (0.90)
  Pallas kernels: 88.3 us -> 78.5 us
    pallas_call x1, Pallas kernels: 37.5 us -> 27.6 us  [message_passing(): pl.pallas_call(functools.partial(message_kernel, num_x, num_y), out_shape...]
where the time goes in v1:
time: 87.5 us; the launch traced here: 87.3 us
  Pallas kernels  78.5 us (90%)
  local copies, waits for them, and re-layouts  7.12 us (8%)
  between operations  1.53 us (2%)
    pallas_call x1, Pallas kernels, mesh_potential(): pl.pallas_call(mesh_kernel, out_shape=(jax.ShapeDtypeStruct((1, 1024), f3...  50.9 us
    pallas_call x1, Pallas kernels, message_passing(): pl.pallas_call(functools.partial(message_kernel, num_x, num_y), out_shape...  27.6 us
    unnamed x37, local copies, waits for them, and re-layouts  4.11 us

profile of v1, /device:TPU:1, one launch (start us, length us, event | category | flops | bytes accessed | tf_op | source)
XLA Modules:
  0.0 87.3 jit_solution(2349101686018962777)
XLA Ops:
  0.6 0.0 copy-start
  0.6 1.1 %fusion = (f32[256,16,8]{0,2,1:T(8,128)S(1)}, f32[256,16,8]{0,2,1:T(8,128)S(1)}) fusion(f32[256,16,16]{0,2,1:T(8,128)} %param.30), kind=kLoop, calls=%fused_computation.2 | loop fusion | bytes 524288 | tf_op jit(solution)/shard_map/slice | solution.py:599
  1.7 0.0 copy-start.1
  1.8 0.1 copy_select_fusion
  1.8 0.0 copy-start.9
  1.9 0.0 copy-start.10
  1.9 0.0 copy-start.11
  1.9 0.1 copy.29.green_ref
  2.6 0.0 copy-start.15
  2.7 0.7 copy-done.15
  3.3 0.0 copy-start.16
  3.3 0.6 copy-done.16
  4.0 0.0 copy-start.13
  4.0 0.0 copy-done
  4.0 0.0 copy-done.1
  4.0 0.0 copy-done.9
  4.0 0.0 copy-done.10
  4.0 0.0 copy-done.11
  4.0 0.6 copy-done.13
  4.7 0.0 copy-start.14
  4.7 0.0 copy-start.4
  4.7 0.0 copy-start.5
  4.7 0.0 copy-start.6
  4.7 0.0 copy-start.7
  4.7 0.0 copy-start.8
  4.7 27.6 %message_passing.1.charges_ref = f32[1,1024]{1,0:T(1,128)S(1)} custom-call(bf16[1024,128]{1,0:T(8,128)(2,1)S(1)} %copy-done.1, bf16[256,1024]{1,0:T(8,128)(2,1)S(1)} %bitcast.15, s32[32,1024]{1,0:T(8,128)S(1)} %copy-done.9, s32[1,1024]{1,0:T(1,128)S(1)} %bitcast.18, s32[1,1024]{1,0:T(1,128)S(1)} %broadcast_in_dim.13.fill_ref, ...), custom_call_target="tpu_custom_call" | custom-call | tf_op jit(solution)/shard_map/message_passing/pallas_call | solution.py:184
  32.3 0.0 copy-start.12
  32.3 0.9 %slice.11 = f32[256,16,1]{0,2,1:T(1,128)S(1)} slice(f32[256,16,16]{0,2,1:T(8,128)} %param.30), slice={[0:256], [0:16], [0:1]} | slice | bytes 32768 | tf_op jit(solution)/shard_map/slice | solution.py:601
  33.3 0.0 copy-start.2
  33.3 0.0 copy-start.3
  33.3 0.1 copy.33
  33.4 0.0 copy-done.14
  33.4 0.0 copy-done.4
  33.4 0.0 copy-done.5
  33.5 0.0 copy-done.6
  33.5 0.0 copy-done.7
  33.5 0.0 copy-done.8
  33.5 0.0 copy-done.12
  33.5 0.7 copy-done.2
  34.2 0.1 copy-done.3
  34.3 50.9 %mesh_potential.1 = (f32[1,1024]{1,0:T(1,128)S(1)}, f32[256,256]{1,0:T(8,128)S(1)}) custom-call(f32[1,1024]{1,0:T(1,128)S(1)} %message_passing.1.charges_ref, s32[1,1024]{1,0:T(1,128)S(1)} %broadcast_in_dim.13.fill_ref, s32[3,1024]{1,0:T(4,128)S(1)} %copy-done.12, f32[12,1024]{1,0:T(8,128)S(1)} %reshape.40.spline_ref, f32[256,128]{1,0:T(8,128)S(1)} %copy.29.green_ref, ...), custom_call_target="tpu_custom_call" | custom-call | tf_op jit(solution)/shard_map/mesh_potential/pallas_call | solution.py:603
  85.2 0.9 copy.37
  86.1 0.6 copy.41
  86.7 0.6 copy.42
  (5 shorter events, 0.0 us)
Async XLA Ops:
  0.6 3.4 %copy-start = (bf16[8,32,1024]{2,1,0:T(8,128)(2,1)S(1)}, bf16[8,32,1024]{2,1,0:T(8,128)(2,1)}, u32[]{:S(2)}) copy-start(bf16[8,32,1024]{2,1,0:T(8,128)(2,1)} %param.20) | copy-start | bytes 1572868
  1.7 2.2 %copy-start.1 = (bf16[1024,128]{1,0:T(8,128)(2,1)S(1)}, bf16[1024,128]{1,0:T(8,128)(2,1)}, u32[]{:S(2)}) copy-start(bf16[1024,128]{1,0:T(8,128)(2,1)} %feats_ref.1) | copy-start | bytes 786436
  1.8 2.2 %copy-start.9 = (s32[32,1024]{1,0:T(8,128)S(1)}, s32[32,1024]{1,0:T(8,128)}, u32[]{:S(2)}) copy-start(s32[32,1024]{1,0:T(8,128)} %nbr_ref.1) | copy-start | bytes 393220
  1.9 2.1 %copy-start.10 = (bf16[2,128,128]{2,1,0:T(8,128)(2,1)S(1)}, bf16[2,128,128]{2,1,0:T(8,128)(2,1)}, u32[]{:S(2)}) copy-start(bf16[2,128,128]{2,1,0:T(8,128)(2,1)} %proj_ref.1) | copy-start | bytes 196612
  1.9 2.1 %copy-start.11 = (bf16[2,128,128]{2,1,0:T(8,128)(2,1)S(1)}, bf16[2,128,128]{2,1,0:T(8,128)(2,1)}, u32[]{:S(2)}) copy-start(bf16[2,128,128]{2,1,0:T(8,128)(2,1)} %mix_ref.1) | copy-start | bytes 196612
  2.6 0.7 copy-start.15
  3.3 0.7 copy-start.16
  4.0 0.7 copy-start.13
  4.7 28.7 %copy-start.14 = (f32[3,4,1024]{2,1,0:T(4,128)S(1)}, f32[3,4,1024]{2,1,0:T(4,128)}, u32[]{:S(2)}) copy-start(f32[3,4,1024]{2,1,0:T(4,128)} %param.25) | copy-start | bytes 147460
  4.7 28.8 %copy-start.4 = (bf16[256,256]{1,0:T(8,128)(2,1)S(1)}, bf16[256,256]{1,0:T(8,128)(2,1)}, u32[]{:S(2)}) copy-start(bf16[256,256]{1,0:T(8,128)(2,1)} %constant.25.clone.ahead_h) | copy-start | bytes 393220
  4.7 28.8 %copy-start.5 = (bf16[256,256]{1,0:T(8,128)(2,1)S(1)}, bf16[256,256]{1,0:T(8,128)(2,1)}, u32[]{:S(2)}) copy-start(bf16[256,256]{1,0:T(8,128)(2,1)} %constant.26.clone.ahead_l) | copy-start | bytes 393220
  4.7 28.8 %copy-start.6 = (bf16[256,256]{1,0:T(8,128)(2,1)S(1)}, bf16[256,256]{1,0:T(8,128)(2,1)}, u32[]{:S(2)}) copy-start(bf16[256,256]{1,0:T(8,128)(2,1)} %constant.27.clone.back_h) | copy-start | bytes 393220
  4.7 28.8 %copy-start.7 = (bf16[256,256]{1,0:T(8,128)(2,1)S(1)}, bf16[256,256]{1,0:T(8,128)(2,1)}, u32[]{:S(2)}) copy-start(bf16[256,256]{1,0:T(8,128)(2,1)} %constant.28.clone.back_l) | copy-start | bytes 393220
  4.7 28.8 %copy-start.8 = (bf16[256,192]{1,0:T(8,128)(2,1)S(1)}, bf16[256,192]{1,0:T(8,128)(2,1)}, u32[]{:S(2)}) copy-start(bf16[256,192]{1,0:T(8,128)(2,1)} %constant.29.clone.fold_ref) | copy-start | bytes 294916
  32.3 1.2 %copy-start.12 = (s32[3,1024]{1,0:T(4,128)S(1)}, s32[3,1024]{1,0:T(4,128)}, u32[]{:S(2)}) copy-start(s32[3,1024]{1,0:T(4,128)} %base_ref.1) | copy-start | bytes 36868
  33.3 1.0 %copy-start.2 = (bf16[512,256]{1,0:T(8,128)(2,1)S(1)}, bf16[512,256]{1,0:T(8,128)(2,1)}, u32[]{:S(2)}) copy-start(bf16[512,256]{1,0:T(8,128)(2,1)} %constant.23.clone.wave_h) | copy-start | bytes 786436
  33.3 1.0 %copy-start.3 = (bf16[512,256]{1,0:T(8,128)(2,1)S(1)}, bf16[512,256]{1,0:T(8,128)(2,1)}, u32[]{:S(2)}) copy-start(bf16[512,256]{1,0:T(8,128)(2,1)} %constant.24.clone.wave_l) | copy-start | bytes 786436

commit v2 on v1

--- a/solution.py
+++ b/solution.py
@@ -215,12 +215,6 @@
         jnp.broadcast_to(w_charge.reshape(1, 128), (8, 128)),
     )
 
-SIDES = ((-1, 0), (1, 0), (0, -1), (0, 1), (-1, -1), (-1, 1), (1, -1), (1, 1))
-SIDE_ROWS = (32, 32, 32, 32, 16, 16, 16, 16)
-SIDE_AT = (0, 32, 64, 96, 128, 144, 160, 176)
-OPPOSITE = (1, 0, 3, 2, 7, 6, 5, 4)
-
-
 def split(values):
     high = values.astype(jnp.bfloat16)
     return high, (values - high.astype(jnp.float32)).astype(jnp.bfloat16)
@@ -243,29 +237,15 @@
     ahead[0, 0], ahead[1, 0] = 1.0, 1.0 - 2.0 * (ids % 2)
     back[0, 0], back[1, 0] = ahead[0, 0], ahead[1, 0]
     back = back / 256.0**3
-    fold = np.zeros((16, 16, 192))
-    for at, (dx, dy) in zip(SIDE_AT, SIDES, strict=True):
-        first_x, first_y = (14 if dx > 0 else 0), (14 if dy > 0 else 0)
-        for i in range(2):
-            if dy == 0:
-                for y in range(16):
-                    fold[y, first_x + i, at + 16 * i + y] = 1
-            elif dx == 0:
-                for x in range(16):
-                    fold[first_y + i, x, at + 16 * i + x] = 1
-            else:
-                for j in range(2):
-                    fold[first_y + j, first_x + i, at + 2 * i + j] = 1
     return (
         *np_split(waves),
         *np_split(ahead.reshape(256, 256)),
         *np_split(back.reshape(256, 256)),
-        fold.reshape(256, 192).astype(ml_dtypes.bfloat16),
     )
 
 
 def regroup(parts):
-    group = lax.broadcasted_iota(jnp.int32, (16, 128), 1) // 16
+    group = lax.broadcasted_iota(jnp.int32, parts[0].shape, 1) // 16
     parts = list(parts)
     for step in (1, 2, 4):
         low = (group & step) == 0
@@ -292,6 +272,42 @@
     return values
 
 
+def turned(values, step):
+    return jnp.concatenate([values[step:], values[:step]], axis=0)
+
+
+def fold_edges(edge):
+    before, after = turned(edge, -1), turned(edge, 1)
+    row = lax.broadcasted_iota(jnp.int32, edge.shape, 1)
+    return [
+        jnp.concatenate(
+            [
+                jnp.where(row < 2, pltpu.roll(before, step, 1), 0.0),
+                jnp.where(row >= 6, pltpu.roll(after, step, 1), 0.0),
+            ],
+            axis=1,
+        )
+        for step in (6, 2)
+    ]
+
+
+def edges_of(real, imag):
+    row = lax.broadcasted_iota(jnp.int32, (16, 8, 128), 1)
+    ends = [
+        pltpu.roll(part, step, 1)
+        for values, step in ((real, 2), (imag, 6))
+        for part in (turned(values, -1)[:, 8:], turned(values, 1)[:, :8])
+    ]
+    return jnp.where(
+        row < 2, ends[0], jnp.where(row < 4, ends[1], jnp.where(row < 6, ends[2], ends[3]))
+    )
+
+
+def tile(low, high=None):
+    high = jnp.zeros_like(low) if high is None else high
+    return jnp.concatenate([low, high], axis=low.ndim - 2).astype(jnp.bfloat16)
+
+
 def profile(cells, base, weights):
     total = jnp.zeros(cells.shape, jnp.float32)
     for offset in range(4):
@@ -312,14 +328,11 @@
     ahead_l,
     back_h,
     back_l,
-    fold_ref,
     atom_ref,
     grid_ref,
     plane,
     prof_h,
     prof_l,
-    halo_out,
-    halo_in,
     z_out,
     z_in,
     y_out,
@@ -329,6 +342,7 @@
     v_out,
     v_in,
     shared,
+    shared_edge,
     green_in,
     send_sem,
     recv_sem,
@@ -343,14 +357,6 @@
         return carry
 
     lax.fori_loop(1, count, greet, 0)
-    for dx, dy in SIDES[4:]:
-        pl.semaphore_signal(
-            barrier,
-            inc=1,
-            device_id=(ring(px, dx, count), ring(py, dy, count)),
-            device_id_type=MESH,
-        )
-
     def remote(source, target, stage, index, where):
         return pltpu.make_async_remote_copy(
             src_ref=source,
@@ -375,18 +381,6 @@
 
         lax.fori_loop(1, count, wait, 0)
 
-    def side_copies(half):
-        return [
-            remote(
-                halo_out.at[half, pl.ds(SIDE_AT[e], SIDE_ROWS[e])],
-                halo_in.at[half, pl.ds(SIDE_AT[OPPOSITE[e]], SIDE_ROWS[e])],
-                half,
-                e,
-                (ring(px, SIDES[e][0], count), ring(py, SIDES[e][1], count)),
-            )
-            for e in range(8)
-        ]
-
     def column_copy(out, into, stage):
         def make(d):
             to = ring(py, d, count)
@@ -401,7 +395,7 @@
 
         return make
 
-    main, extra = pl.ds(0, 2), pl.ds(2, 1)
+    main, extra = pl.ds(0, 3), pl.ds(3, 2)
 
     def green_copy():
         return remote(green_last_ref, green_in, 8, 0, (px, 0))
@@ -424,76 +418,96 @@
     edge_x, edge_y = (profile(edge, *rows(dim)) for dim in (0, 1))
     for y in range(16):
         plane[16 * y : 16 * y + 16, :] = in_y[y : y + 1, :] * in_x
+    for y in range(16):
+        plane[256 + 8 * y : 264 + 8 * y, :] = in_y[y : y + 1, :] * edge_x
     for i in range(4):
-        at = 256 + 32 * (i // 2) + 16 * (i % 2)
-        plane[at : at + 16, :] = edge_x[i : i + 1, :] * in_y
-        plane[at + 64 : at + 80, :] = edge_y[i : i + 1, :] * in_x
-    corner = sixteen < 4
-    corner_x = [
-        profile(jnp.where(corner, sixteen // 2 + begin, 99), *rows(0)) for begin in (0, 18)
-    ]
-    corner_y = [
-        profile(jnp.where(corner, sixteen % 2 + begin, 99), *rows(1)) for begin in (0, 18)
-    ]
-    for e in range(4):
-        at = 256 + SIDE_AT[4 + e]
-        plane[at : at + 16, :] = corner_x[e // 2] * corner_y[e % 2]
+        plane[384 + 16 * i : 400 + 16 * i, :] = edge_y[i : i + 1, :] * in_x
+        plane[448 + 8 * i : 456 + 8 * i, :] = edge_y[i : i + 1, :] * edge_x
 
     high, low = split(plane[...] * charges_ref[...])
     spread = dot(high, prof_h[...], NT) + dot(low, prof_h[...], NT) + dot(high, prof_l[...], NT)
-    halo_out[0] = spread[256:].astype(jnp.bfloat16)
-    pl.semaphore_wait(barrier, 34)
-    copies = side_copies(0)
-    for copy in copies:
-        copy.start()
-
-    @pl.when(py == 8)
-    def _():
-        green_copy().start()
-
-    for copy in copies:
-        copy.wait()
-    high, low = split(spread[:256] + dot(fold_ref[...], halo_in[0]))
+    edges = spread[256:]
+    edges = [
+        tile(edges[:128].reshape(16, 8, 256)).reshape(256, 256),
+        tile(edges[128:192]),
+        tile(tile(edges[192:].reshape(4, 8, 256)).reshape(64, 256)),
+    ]
+    edges = jnp.concatenate(edges, axis=0)
+    high, low = split(spread[:256])
 
     lines = dot(ahead_h[...], high, NT) + dot(ahead_l[...], high, NT) + dot(ahead_h[...], low, NT)
     halves = [
         swap_groups(lines[:, 128 * half : 128 * half + 128].reshape(32, 8, 128)) for half in (0, 1)
     ]
-    z_out[...] = jnp.concatenate(halves, axis=1).astype(jnp.bfloat16).reshape(2, 16, 16, 128)
+    z_out[0:2] = jnp.concatenate(halves, axis=1).astype(jnp.bfloat16).reshape(2, 16, 16, 128)
+    lines = dot(ahead_h[...], edges, NT) + dot(ahead_l[...], edges, NT)
+    real, imag = lines[:128], lines[128:]
+    sides = real[:, :256] + pltpu.roll(imag[:, :256], 4, 1)
+    ends = real[:, 256:384] + pltpu.roll(imag[:, 256:384], 64, 1)
+    corners = real[:, 384:] + pltpu.roll(imag[:, 384:], 4, 1)
+    pieces = [
+        swap_groups(part.reshape(16, 8, 128))
+        for part in (sides[:, :128], sides[:, 128:], ends, corners)
+    ]
+    z_out[2] = tile(pieces[0], pieces[1])
+    z_out[3] = tile(pieces[2], pieces[3])
+    pl.semaphore_wait(barrier, 30)
     make = column_copy(z_out, z_in, 2)
     exchange(make)
+
+    @pl.when(py == 8)
+    def _():
+        green_copy().start()
+
     z_in[:, pl.ds(py, 1)] = z_out[:, pl.ds(py, 1)]
     arrive(make)
 
     cos_h, sin_h = wave_h[:256], wave_h[256:]
     cos_l, sin_l = wave_l[:256], wave_l[256:]
-    both = jnp.concatenate([z_in[0].reshape(256, 128), z_in[1].reshape(256, 128)], axis=1)
-    both = jnp.transpose(both.astype(jnp.float32)).astype(jnp.bfloat16)
+    ends = z_in[3].astype(jnp.float32)
+    adds = [*fold_edges(ends[:, :8]), fold_edges(ends[:, 8:])[0]]
+    both = jnp.concatenate(
+        [(z_in[i].astype(jnp.float32) + adds[i]).reshape(256, 128) for i in range(3)], axis=1
+    )
+    both = jnp.transpose(both).astype(jnp.bfloat16)
     c = dot(both, cos_h) + dot(both, cos_l)
     s = dot(both, sin_h) + dot(both, sin_l)
     apart = (lax.broadcasted_iota(jnp.int32, (128, 256), 0) < 16) & (py == 0)
-    real = c[:128] + jnp.where(apart, 0.0, s[128:])
-    imag = jnp.where(apart, 0.0, c[128:]) - s[:128]
+    real = c[:128] + jnp.where(apart, 0.0, s[128:256])
+    imag = jnp.where(apart, 0.0, c[128:256]) - s[:128]
+
+    c_edge, s_edge = (v[256:].reshape(8, 16, 256)[:, :8] for v in (c, s))
+    c_swap, s_swap = pltpu.roll(c_edge, 4, 1), pltpu.roll(s_edge, 4, 1)
+    top = lax.broadcasted_iota(jnp.int32, (8, 8, 256), 1) < 4
+    apart = (lax.broadcasted_iota(jnp.int32, (8, 8, 256), 0) == 0) & (py == 0)
+    edge = jnp.where(
+        top,
+        c_edge + jnp.where(apart, 0.0, s_swap),
+        jnp.where(apart, 0.0, c_edge) - s_swap,
+    )
 
     def to_slots(values, layer):
         for half in (0, 1):
             lanes = slice(128 * half, 128 * half + 128)
-            done = regroup([values[16 * i : 16 * i + 16, lanes] for i in range(8)])
+            done = regroup([v[:, lanes] for v in values])
             for i in range(8):
-                y_out[layer, 8 * half + i] = done[i].astype(jnp.bfloat16)
-
-    to_slots(real, 0)
-    to_slots(imag, 1)
+                whole = done[i].shape[0] == 16
+                y_out[layer, 8 * half + i] = done[i].astype(jnp.bfloat16) if whole else tile(done[i])
+
+    to_slots([real[16 * i : 16 * i + 16] for i in range(8)], 0)
+    to_slots([imag[16 * i : 16 * i + 16] for i in range(8)], 1)
+    to_slots([edge[i] for i in range(8)], 2)
     make = row_copy(y_out, y_in, 3, main)
     exchange(make)
-    y_in[0:2, pl.ds(px, 1)] = y_out[0:2, pl.ds(px, 1)]
+    y_in[0:3, pl.ds(px, 1)] = y_out[0:3, pl.ds(px, 1)]
 
     @pl.when(py == 0)
     def _():
-        blank = jnp.zeros((96, 256), jnp.float32)
-        to_slots(jnp.concatenate([c[128:144], -s[128:144], blank], axis=0), 2)
+        blank = jnp.zeros((16, 256), jnp.float32)
+        to_slots([c[128:144], -s[128:144]] + [blank] * 6, 3)
+        to_slots([jnp.where(top[0], c_swap[0], -s_edge[0])] + [blank[:8]] * 7, 4)
         exchange(row_copy(y_out, y_in, 4, extra))
-        y_in[2:3, pl.ds(px, 1)] = y_out[2:3, pl.ds(px, 1)]
+        y_in[3:5, pl.ds(px, 1)] = y_out[3:5, pl.ds(px, 1)]
 
     arrive(make)
 
@@ -507,33 +521,42 @@
             dot(sin_h, high) + dot(sin_l, high) + dot(sin_h, low),
         )
 
+    adds = fold_edges(y_in[2].astype(jnp.float32)[:, :8])
     c, s = forward_x(
-        jnp.concatenate([y_in[0].reshape(256, 128), y_in[1].reshape(256, 128)], axis=1)
+        jnp.concatenate(
+            [(y_in[i].astype(jnp.float32) + adds[i]).reshape(256, 128) for i in range(2)], axis=1
+        ).astype(jnp.bfloat16)
     )
     real = (c[:, :128] + s[:, 128:]) * green_ref[...]
     imag = (c[:, 128:] - s[:, :128]) * green_ref[...]
     c, s = inverse_x(jnp.concatenate([real, imag], axis=1))
-    x_out[0] = (c[:, :128] - s[:, 128:]).astype(jnp.bfloat16).reshape(16, 16, 128)
-    x_out[1] = (c[:, 128:] + s[:, :128]).astype(jnp.bfloat16).reshape(16, 16, 128)
+    real = (c[:, :128] - s[:, 128:]).reshape(16, 16, 128)
+    imag = (c[:, 128:] + s[:, :128]).reshape(16, 16, 128)
+    x_out[0] = real.astype(jnp.bfloat16)
+    x_out[1] = imag.astype(jnp.bfloat16)
+    x_out[2] = tile(edges_of(real, imag))
     make = row_copy(x_out, x_in, 5, main)
     exchange(make)
-    x_in[0:2, pl.ds(px, 1)] = x_out[0:2, pl.ds(px, 1)]
+    x_in[0:3, pl.ds(px, 1)] = x_out[0:3, pl.ds(px, 1)]
 
     @pl.when(py == 0)
     def _():
         arrive(row_copy(y_out, y_in, 4, extra))
         green_copy().wait_recv()
         first = lax.broadcasted_iota(jnp.int32, (256, 128), 1) < 16
-        c, s = forward_x(y_in[2].reshape(256, 128))
+        adds = fold_edges(y_in[4].astype(jnp.float32)[:, :8])
+        last = y_in[3].astype(jnp.float32) + adds[0] + pltpu.roll(adds[1], 16, 2)
+        c, s = forward_x(last.reshape(256, 128).astype(jnp.bfloat16))
         real = (c + pltpu.roll(s, 112, 1)) * green_in[...]
         imag = (pltpu.roll(c, 112, 1) - s) * green_in[...]
         c, s = inverse_x(real + pltpu.roll(imag, 16, 1))
         real = jnp.where(first, c - pltpu.roll(s, 112, 1), 0.0)
         imag = jnp.where(first, pltpu.roll(c, 112, 1) + s, 0.0)
-        x_out[2] = (real + pltpu.roll(imag, 16, 1)).astype(jnp.bfloat16).reshape(16, 16, 128)
+        x_out[3] = (real + pltpu.roll(imag, 16, 1)).astype(jnp.bfloat16).reshape(16, 16, 128)
+        x_out[4] = tile(edges_of(real.reshape(16, 16, 128), imag.reshape(16, 16, 128)))
         back_copy = row_copy(x_out, x_in, 6, extra)
         exchange(back_copy)
-        x_in[2:3, pl.ds(px, 1)] = x_out[2:3, pl.ds(px, 1)]
+        x_in[3:5, pl.ds(px, 1)] = x_out[3:5, pl.ds(px, 1)]
 
     @pl.when(py == 8)
     def _():
@@ -541,23 +564,26 @@
 
     arrive(make)
 
-    def to_rows(layer):
+    def to_rows(layer, count=16):
         halves = [
-            regroup([x_in[layer, 8 * half + i].astype(jnp.float32) for i in range(8)])
+            regroup([x_in[layer, 8 * half + i].astype(jnp.float32)[:count] for i in range(8)])
             for half in (0, 1)
         ]
         return [jnp.concatenate([halves[0][i], halves[1][i]], axis=1) for i in range(8)]
 
-    real, imag = to_rows(0), to_rows(1)
+    real, imag, edge = to_rows(0), to_rows(1), to_rows(2, 8)
     shared[0] = real[0]
     shared[1] = imag[0]
+    shared_edge[...] = edge[0]
 
     @pl.when(py == 0)
     def _():
         arrive(row_copy(x_out, x_in, 6, extra))
-        last = to_rows(2)
+        last = to_rows(3)
         shared[0] = -last[1]
         shared[1] = last[0]
+        last = pltpu.roll(to_rows(4, 8)[0], 4, 0)
+        shared_edge[...] = jnp.where(top[0], -last, last)
 
     a = jnp.concatenate(real, axis=0).astype(jnp.bfloat16)
     b = jnp.concatenate(imag, axis=0).astype(jnp.bfloat16)
@@ -565,30 +591,66 @@
     b_too = jnp.concatenate([shared[1], *imag[1:]], axis=0).astype(jnp.bfloat16)
     real = dot(cos_h, a, NT) + dot(cos_l, a, NT) - dot(sin_h, b, NT) - dot(sin_l, b, NT)
     imag = dot(cos_h, b_too, NT) + dot(cos_l, b_too, NT) + dot(sin_h, a_too, NT) + dot(sin_l, a_too, NT)
-    v_out[0] = real.astype(jnp.bfloat16).reshape(16, 16, 128)
-    v_out[1] = imag.astype(jnp.bfloat16).reshape(16, 16, 128)
+    sides = []
+    for first in (edge[0], shared_edge[...]):
+        rows = jnp.concatenate([tile(v) for v in [first, *edge[1:]]], axis=0)
+        sides.append(
+            (
+                dot(cos_h, rows, NT) + dot(cos_l, rows, NT),
+                dot(sin_h, rows, NT) + dot(sin_l, rows, NT),
+            )
+        )
+    within = lax.broadcasted_iota(jnp.int32, (256, 128), 1) % 16
+    sides = jnp.where(
+        within < 4,
+        sides[0][0] - pltpu.roll(sides[0][1], 124, 1),
+        sides[1][0] + pltpu.roll(sides[1][1], 4, 1),
+    )
+    sides = jnp.where(within < 8, sides, 0.0).reshape(16, 16, 128)
+    real, imag = real.reshape(16, 16, 128), imag.reshape(16, 16, 128)
+    v_out[0] = real.astype(jnp.bfloat16)
+    v_out[1] = imag.astype(jnp.bfloat16)
+    v_out[2] = sides.astype(jnp.bfloat16)
+    v_out[3] = tile(edges_of(real, imag), edges_of(sides, sides))
     make = column_copy(v_out, v_in, 7)
     exchange(make)
     v_in[:, pl.ds(py, 1)] = v_out[:, pl.ds(py, 1)]
     arrive(make)
 
-    got = v_in[...].reshape(32, 16, 128).astype(jnp.float32)
-    halves = [swap_groups(got[:, 8 * half : 8 * half + 8]).reshape(256, 128) for half in (0, 1)]
-    lines = jnp.concatenate(halves, axis=1).astype(jnp.bfloat16)
+    def to_lines(values):
+        return swap_groups(values).reshape(-1, 128)
+
+    got = v_in[0:2].reshape(32, 16, 128).astype(jnp.float32)
+    lines = jnp.concatenate([to_lines(got[:, :8]), to_lines(got[:, 8:])], axis=1).astype(jnp.bfloat16)
     grid = dot(lines, back_h[...], TN) + dot(lines, back_l[...], TN)
     grid_ref[...] = grid
-    high, low = split(grid)
-    halo_out[1] = dot(fold_ref[...], high, TN).astype(jnp.bfloat16)
-    copies = side_copies(1)
-    for copy in copies:
-        copy.start()
-
+    got = v_in[2:4].reshape(32, 16, 128).astype(jnp.float32)
+    sides = jnp.concatenate([to_lines(got[:16, :8]), to_lines(got[:16, 8:])], axis=1)
+    ends, corners = to_lines(got[16:, :8]), to_lines(got[16:, 8:])
+    lines = jnp.concatenate(
+        [
+            jnp.concatenate([sides, ends, corners], axis=1),
+            jnp.concatenate(
+                [pltpu.roll(sides, 252, 1), pltpu.roll(ends, 64, 1), pltpu.roll(corners, 124, 1)],
+                axis=1,
+            ),
+        ],
+        axis=0,
+    ).astype(jnp.bfloat16)
+    edges = dot(lines, back_h[...], TN) + dot(lines, back_l[...], TN)
+
+    values = jnp.concatenate(
+        [
+            grid,
+            edges[:256].reshape(16, 16, 256)[:, :8].reshape(128, 256),
+            edges[256:320],
+            edges[384:448].reshape(4, 16, 256)[:, :8].reshape(32, 256),
+        ],
+        axis=0,
+    )
+    high, low = split(values)
     sampled = dot(high, prof_h[...]) + dot(low, prof_h[...]) + dot(high, prof_l[...])
-    total = jnp.sum(sampled * plane[:256], axis=0, keepdims=True)
-    for copy in copies:
-        copy.wait()
-    sampled = dot(halo_in[1], prof_h[...]) + dot(halo_in[1], prof_l[...])
-    total = total + jnp.sum(sampled * plane[256:], axis=0, keepdims=True)
+    total = jnp.sum(sampled * plane[...], axis=0, keepdims=True)
     inside = lax.broadcasted_iota(jnp.int32, (1, 1024), 1) < fill_ref[...]
     atom_ref[...] = jnp.where(inside, total, 0.0)
 
@@ -606,23 +668,22 @@
             jax.ShapeDtypeStruct((1, 1024), f32),
             jax.ShapeDtypeStruct((256, 256), f32),
         ),
-        in_specs=[vmem] * 13,
+        in_specs=[vmem] * 12,
         out_specs=(vmem, vmem),
         scratch_shapes=[
-            pltpu.VMEM((448, 1024), f32),
+            pltpu.VMEM((480, 1024), f32),
             pltpu.VMEM((256, 1024), bf16),
             pltpu.VMEM((256, 1024), bf16),
-            pltpu.VMEM((2, 192, 256), bf16),
-            pltpu.VMEM((2, 192, 256), bf16),
-            pltpu.VMEM((2, *blocks), bf16),
-            pltpu.VMEM((2, *blocks), bf16),
-            pltpu.VMEM((3, *blocks), bf16),
-            pltpu.VMEM((3, *blocks), bf16),
-            pltpu.VMEM((3, *blocks), bf16),
-            pltpu.VMEM((3, *blocks), bf16),
-            pltpu.VMEM((2, *blocks), bf16),
-            pltpu.VMEM((2, *blocks), bf16),
+            pltpu.VMEM((4, *blocks), bf16),
+            pltpu.VMEM((4, *blocks), bf16),
+            pltpu.VMEM((5, *blocks), bf16),
+            pltpu.VMEM((5, *blocks), bf16),
+            pltpu.VMEM((5, *blocks), bf16),
+            pltpu.VMEM((5, *blocks), bf16),
+            pltpu.VMEM((4, *blocks), bf16),
+            pltpu.VMEM((4, *blocks), bf16),
             pltpu.VMEM((2, 16, 256), f32),
+            pltpu.VMEM((8, 256), f32),
             pltpu.VMEM((256, 128), f32),
             pltpu.SemaphoreType.DMA((9, 16)),
             pltpu.SemaphoreType.DMA((9, 16)),

time: 87.5 us -> 79 us (0.903)
  Pallas kernels: 78.5 us -> 69.4 us
    pallas_call x1, Pallas kernels: 50.9 us -> 41.8 us  [mesh_potential(): pl.pallas_call(mesh_kernel, out_shape=(jax.ShapeDtypeStruct((1, 1024), f3...]
    unnamed x37 -> x35, local copies, waits for them, and re-layouts: 4.11 us -> 4.12 us
where the time goes in v2:
time: 79 us; the launch traced here: 78.1 us
  Pallas kernels  69.4 us (88%)
  local copies, waits for them, and re-layouts  7.13 us (9%)
  between operations  1.52 us (2%)
    pallas_call x1, Pallas kernels, mesh_potential(): pl.pallas_call(mesh_kernel, out_shape=(jax.ShapeDtypeStruct((1, 1024), f3...  41.8 us
    pallas_call x1, Pallas kernels, message_passing(): pl.pallas_call(functools.partial(message_kernel, num_x, num_y), out_shape...  27.6 us
    unnamed x35, local copies, waits for them, and re-layouts  4.12 us

profile of v2, /device:TPU:1, one launch (start us, length us, event | category | flops | bytes accessed | tf_op | source)
XLA Modules:
  0.0 78.1 jit_solution(13874157243016254259)
XLA Ops:
  0.6 0.0 copy-start
  0.6 1.1 %fusion = (f32[256,16,8]{0,2,1:T(8,128)S(1)}, f32[256,16,8]{0,2,1:T(8,128)S(1)}) fusion(f32[256,16,16]{0,2,1:T(8,128)} %param.29), kind=kLoop, calls=%fused_computation.2 | loop fusion | bytes 524288 | tf_op jit(solution)/shard_map/slice | solution.py:661
  1.7 0.0 copy-start.1
  1.8 0.1 copy_select_fusion
  1.8 0.0 copy-start.4
  1.9 0.0 copy-start.9
  1.9 0.0 copy-start.10
  1.9 0.1 copy.28.green_ref
  2.6 0.0 copy-start.14
  2.7 0.7 copy-done.14
  3.3 0.0 copy-start.15
  3.3 0.6 copy-done.15
  4.0 0.0 copy-start.12
  4.0 0.0 copy-done
  4.0 0.0 copy-done.1
  4.0 0.0 copy-done.4
  4.0 0.0 copy-done.9
  4.0 0.0 copy-done.10
  4.0 0.6 copy-done.12
  4.7 0.0 copy-start.13
  4.7 0.0 copy-start.5
  4.7 0.0 copy-start.6
  4.7 0.0 copy-start.7
  4.7 0.0 copy-start.8
  4.7 27.6 %message_passing.1.charges_ref = f32[1,1024]{1,0:T(1,128)S(1)} custom-call(bf16[1024,128]{1,0:T(8,128)(2,1)S(1)} %copy-done.1, bf16[256,1024]{1,0:T(8,128)(2,1)S(1)} %bitcast.15, s32[32,1024]{1,0:T(8,128)S(1)} %copy-done.4, s32[1,1024]{1,0:T(1,128)S(1)} %bitcast.18, s32[1,1024]{1,0:T(1,128)S(1)} %broadcast_in_dim.13.fill_ref, ...), custom_call_target="tpu_custom_call" | custom-call | tf_op jit(solution)/shard_map/message_passing/pallas_call | solution.py:184
  32.3 0.0 copy-start.11
  32.3 0.9 %slice.11 = f32[256,16,1]{0,2,1:T(1,128)S(1)} slice(f32[256,16,16]{0,2,1:T(8,128)} %param.29), slice={[0:256], [0:16], [0:1]} | slice | bytes 32768 | tf_op jit(solution)/shard_map/slice | solution.py:663
  33.2 0.0 copy-start.2
  33.2 0.0 copy-start.3
  33.3 0.1 copy.32
  33.4 0.0 copy-done.13
  33.4 0.0 copy-done.5
  33.4 0.0 copy-done.6
  33.4 0.0 copy-done.7
  33.5 0.0 copy-done.8
  33.5 0.0 copy-done.11
  33.5 0.7 copy-done.2
  34.2 0.1 copy-done.3
  34.3 41.8 %mesh_potential.1 = (f32[1,1024]{1,0:T(1,128)S(1)}, f32[256,256]{1,0:T(8,128)S(1)}) custom-call(f32[1,1024]{1,0:T(1,128)S(1)} %message_passing.1.charges_ref, s32[1,1024]{1,0:T(1,128)S(1)} %broadcast_in_dim.13.fill_ref, s32[3,1024]{1,0:T(4,128)S(1)} %copy-done.11, f32[12,1024]{1,0:T(8,128)S(1)} %reshape.40.spline_ref, f32[256,128]{1,0:T(8,128)S(1)} %copy.28.green_ref, ...), custom_call_target="tpu_custom_call" | custom-call | tf_op jit(solution)/shard_map/mesh_potential/pallas_call | solution.py:665
  76.0 0.9 %copy.36 = f32[16,16,256]{2,0,1:T(8,128)} copy(f32[16,16,256]{2,1,0:T(8,128)S(1)} %bitcast.16) | data formatting | bytes 524288 | tf_op jit(solution)/shard_map/reshape | solution.py:704
  76.9 0.6 copy.40
  77.5 0.6 copy.41
  (5 shorter events, 0.0 us)
Async XLA Ops:
  0.6 3.4 %copy-start = (bf16[8,32,1024]{2,1,0:T(8,128)(2,1)S(1)}, bf16[8,32,1024]{2,1,0:T(8,128)(2,1)}, u32[]{:S(2)}) copy-start(bf16[8,32,1024]{2,1,0:T(8,128)(2,1)} %param.19) | copy-start | bytes 1572868
  1.7 2.2 %copy-start.1 = (bf16[1024,128]{1,0:T(8,128)(2,1)S(1)}, bf16[1024,128]{1,0:T(8,128)(2,1)}, u32[]{:S(2)}) copy-start(bf16[1024,128]{1,0:T(8,128)(2,1)} %feats_ref.1) | copy-start | bytes 786436
  1.8 2.2 %copy-start.4 = (s32[32,1024]{1,0:T(8,128)S(1)}, s32[32,1024]{1,0:T(8,128)}, u32[]{:S(2)}) copy-start(s32[32,1024]{1,0:T(8,128)} %nbr_ref.1) | copy-start | bytes 393220
  1.9 2.1 %copy-start.9 = (bf16[2,128,128]{2,1,0:T(8,128)(2,1)S(1)}, bf16[2,128,128]{2,1,0:T(8,128)(2,1)}, u32[]{:S(2)}) copy-start(bf16[2,128,128]{2,1,0:T(8,128)(2,1)} %proj_ref.1) | copy-start | bytes 196612
  1.9 2.1 %copy-start.10 = (bf16[2,128,128]{2,1,0:T(8,128)(2,1)S(1)}, bf16[2,128,128]{2,1,0:T(8,128)(2,1)}, u32[]{:S(2)}) copy-start(bf16[2,128,128]{2,1,0:T(8,128)(2,1)} %mix_ref.1) | copy-start | bytes 196612
  2.6 0.7 copy-start.14
  3.3 0.7 copy-start.15
  4.0 0.7 copy-start.12
  4.7 28.7 %copy-start.13 = (f32[3,4,1024]{2,1,0:T(4,128)S(1)}, f32[3,4,1024]{2,1,0:T(4,128)}, u32[]{:S(2)}) copy-start(f32[3,4,1024]{2,1,0:T(4,128)} %param.24) | copy-start | bytes 147460
  4.7 28.8 %copy-start.5 = (bf16[256,256]{1,0:T(8,128)(2,1)S(1)}, bf16[256,256]{1,0:T(8,128)(2,1)}, u32[]{:S(2)}) copy-start(bf16[256,256]{1,0:T(8,128)(2,1)} %constant.23.clone.ahead_h) | copy-start | bytes 393220
  4.7 28.8 %copy-start.6 = (bf16[256,256]{1,0:T(8,128)(2,1)S(1)}, bf16[256,256]{1,0:T(8,128)(2,1)}, u32[]{:S(2)}) copy-start(bf16[256,256]{1,0:T(8,128)(2,1)} %constant.24.clone.ahead_l) | copy-start | bytes 393220
  4.7 28.8 %copy-start.7 = (bf16[256,256]{1,0:T(8,128)(2,1)S(1)}, bf16[256,256]{1,0:T(8,128)(2,1)}, u32[]{:S(2)}) copy-start(bf16[256,256]{1,0:T(8,128)(2,1)} %constant.25.clone.back_h) | copy-start | bytes 393220
  4.7 28.8 %copy-start.8 = (bf16[256,256]{1,0:T(8,128)(2,1)S(1)}, bf16[256,256]{1,0:T(8,128)(2,1)}, u32[]{:S(2)}) copy-start(bf16[256,256]{1,0:T(8,128)(2,1)} %constant.26.clone.back_l) | copy-start | bytes 393220
  32.3 1.2 %copy-start.11 = (s32[3,1024]{1,0:T(4,128)S(1)}, s32[3,1024]{1,0:T(4,128)}, u32[]{:S(2)}) copy-start(s32[3,1024]{1,0:T(4,128)} %base_ref.1) | copy-start | bytes 36868
  33.2 1.0 %copy-start.2 = (bf16[512,256]{1,0:T(8,128)(2,1)S(1)}, bf16[512,256]{1,0:T(8,128)(2,1)}, u32[]{:S(2)}) copy-start(bf16[512,256]{1,0:T(8,128)(2,1)} %constant.21.clone.wave_h) | copy-start | bytes 786436
  33.2 1.0 %copy-start.3 = (bf16[512,256]{1,0:T(8,128)(2,1)S(1)}, bf16[512,256]{1,0:T(8,128)(2,1)}, u32[]{:S(2)}) copy-start(bf16[512,256]{1,0:T(8,128)(2,1)} %constant.22.clone.wave_l) | copy-start | bytes 786436
